TPU v7x, 32 devices: a whole 2x2x4 slice. The times are simulated.
32 devices in a mesh: groups: 2 (over x), dp: 16 (over z, y, core).
Axes of the slice: x: 2, y: 2, z: 4, core: 2. Of those that a mesh axis runs over, the one named last changes fastest.
Arguments:
- queries: bfloat16 [32, 2, 4096], P('dp'), may hold values from -6 to 6
- inv_hessian: bfloat16 [2, 4096, 4096], P(None, 'dp'), as said below
- train_grads: bfloat16 [16384, 2, 4096], P(('groups', 'dp')), parts along dimension 0, may hold values from -0.0625 to 0.0625
Outputs:
- scores: float32 [32, 16384], P(None, ('groups', 'dp')), parts along dimension 1
There are 2 independent parts, one for each index of `groups`. A program takes and returns all parts, laid end to end along the dimension named above; an argument that names none is the same for every part. Nothing has to cross between parts.
Inputs may be any that keep to these rules, and one draw needn't show every extreme that they name: Each inv_hessian[l] is symmetric.
All inputs are finite; a program needn't handle non-finite values.
Results may differ from a plain program's by a relative error of at most 0.0029.
Values may be sent and summed in bfloat16 or wider, within the bound.
A program may use at most 128 MiB of HBM per device.

v0:
```python
import jax
import jax.numpy as jnp
from jax import lax
from jax.sharding import PartitionSpec as P


def per_device(queries, inv_hessian, train_grads):
    query_count, layer_count, feature_count = queries.shape
    train_count = train_grads.shape[0]
    train_flat = train_grads.reshape(train_count, layer_count * feature_count)
    query_slices = lax.all_to_all(queries, "dp", split_axis=2, concat_axis=0, tiled=True)
    precond = lax.psum_scatter(
        jnp.einsum("qlk,lkj->qlj", query_slices, inv_hessian, preferred_element_type=jnp.float32),
        "dp",
        scatter_dimension=0,
        tiled=True,
    ).astype(jnp.bfloat16)
    gathered_piece = lax.all_gather(precond, "dp", axis=0, tiled=True)
    flat_piece = gathered_piece.reshape(gathered_piece.shape[0], layer_count * feature_count)
    return jnp.dot(flat_piece, train_flat.T, preferred_element_type=jnp.float32)


def solution(mesh):
    return jax.shard_map(
        per_device,
        mesh=mesh,
        in_specs=(P("dp", None, None), P(None, "dp", None), P(("groups", "dp"), None, None)),
        out_specs=P(None, ("groups", "dp")),
        check_vma=False,
    )
```

profile of v0, /device:TPU:0, one launch (start us, length us, event | category | flops | bytes accessed | tf_op | source)
XLA Modules:
  0.0 132.7 jit_solution(16172447502031639619)
XLA Ops:
  0.0 0.0 copy-start
  0.0 4.3 %copy.7 = bf16[2,2,4096]{1,0,2:T(2,128)(2,1)S(1)} copy(bf16[2,2,4096]{2,1,0:T(2,128)(2,1)} %param.3) | data formatting | bytes 65536 | tf_op args[0]
  4.3 3.8 %reshape.6 = bf16[16,2,512]{2,1,0:T(2,128)(2,1)} reshape(bf16[4096,2,2]{2,1,0:T(2,128)(2,1)S(1)} %bitcast.13) | data formatting | bytes 65536
  8.2 7.4 %all-to-all-start = ((bf16[16,2,512]{2,1,0:T(2,128)(2,1)}), bf16[16,2,512]{2,1,0:T(2,128)(2,1)S(1)}, u32[]{:S(2)}, u32[]{:S(2)}) async-start(bf16[16,2,512]{2,1,0:T(2,128)(2,1)} %reshape.6), calls=%async_computation | async-start | bytes 65536 | tf_op jit(solution)/shard_map/all_to_all | solution.py:11
  15.6 0.0 copy-done
  15.6 0.6 dynamic-slice
  16.7 5.5 %all-to-all-done = bf16[16,2,512]{2,1,0:T(2,128)(2,1)S(1)} async-done(((bf16[16,2,512]{2,1,0:T(2,128)(2,1)}), bf16[16,2,512]{2,1,0:T(2,128)(2,1)S(1)}, u32[]{:S(2)}, u32[]{:S(2)}) %all-to-all-start) | async-done | bytes 32800 | tf_op jit(solution)/shard_map/all_to_all | solution.py:11
  22.2 4.5 %reshape.7 = bf16[4096,2,2]{2,1,0:T(2,128)(2,1)S(1)} reshape(bf16[16,2,512]{2,1,0:T(2,128)(2,1)S(1)} %all-to-all-done) | data formatting | bytes 65536
  26.7 1.3 %copy.8 = bf16[2,2,16,256]{3,1,0,2:T(2,128)(2,1)S(1)} copy(bf16[2,2,16,256]{1,0,3,2:T(2,128)(2,1)S(1)} %bitcast.12) | data formatting | bytes 65536 | tf_op jit(solution)/shard_map/all_to_all | solution.py:11
  28.1 3.0 %convolution_bitcast_fusion = f32[32,2,4096]{2,0,1:T(8,128)S(1)} fusion(bf16[2,256,4096]{2,1,0:T(8,128)(2,1)} %param.4, bf16[32,2,256]{2,1,0:T(2,128)(2,1)S(1)} %bitcast.14), kind=kOutput, calls=%fused_computation.2 | convolution fusion | flops 134217728 | bytes 5275648 | tf_op jit(solution)/shard_map/qlk,lkj->qlj/dot_general | solution.py:13
  31.1 69.3 %all-reduce.2 = bf16[32,2,4096]{2,0,1:T(8,128)(2,1)S(1)} all-reduce(f32[32,2,4096]{2,0,1:T(8,128)S(1)} %convolution_bitcast_fusion), channel_id=2, replica_groups=mesh['groups'=2,'dp'=16] {'dp'}, use_global_device_ids=true, to_apply=%region_0.0.clone | all-reduce | flops 262144 | bytes 1572864
  100.5 18.9 %all_gather.3 = bf16[32,2,4096]{2,1,0:T(2,128)(2,1)S(1)} all-gather(bf16[2,2,4096]{2,1,0:T(2,128)(2,1)S(1)} %copy.10), channel_id=1, replica_groups=mesh['groups'=2,'dp'=16] {'dp'}, dimensions={0}, use_global_device_ids=true | all-gather | bytes 557056 | tf_op jit(solution)/shard_map/all_gather | solution.py:18
  119.4 13.3 %fusion.2 = f32[32,512]{1,0:T(8,128)} fusion(bf16[512,2,4096]{2,1,0:T(2,128)(2,1)} %param.5, bf16[32,2,4096]{2,1,0:T(2,128)(2,1)S(1)} %all_gather.3), kind=kOutput, calls=%fused_computation.3 | convolution fusion | flops 268435456 | bytes 8978432 | tf_op jit(solution)/shard_map/dot_general | solution.py:20
  (2 shorter events, 0.1 us)
Async XLA Ops:
  0.0 15.6 %copy-start = (u32[32]{0:T(128)S(1)}, u32[32]{0:T(128)}, u32[]{:S(2)}) copy-start(u32[32]{0:T(128)} %constant.3) | copy-start | bytes 388
  8.2 14.0 %all-to-all-start = ((bf16[16,2,512]{2,1,0:T(2,128)(2,1)}), bf16[16,2,512]{2,1,0:T(2,128)(2,1)S(1)}, u32[]{:S(2)}, u32[]{:S(2)}) async-start(bf16[16,2,512]{2,1,0:T(2,128)(2,1)} %reshape.6), calls=%async_computation | async-start | bytes 65536 | tf_op jit(solution)/shard_map/all_to_all | solution.py:11
where the time goes:
time: 133 us
  blocking collectives  88.2 us (66%)
  matrix products  16.3 us (12%)
  local copies, waits for them, and re-layouts  14.7 us (11%)
  starting transfers between devices  7.39 us (6%)
  waiting for transfers between devices  5.48 us (4%)
    unnamed x1, blocking collectives  69.3 us
    all_gather x1, blocking collectives, per_device(): gathered_piece = lax.all_gather(precond, 'dp', axis=0, tiled=True)  18.9 us
    dot_general x1, matrix products, per_device(): return jnp.dot(flat_piece, train_flat.T, preferred_element_type=jnp.float32)  13.3 us
    unnamed x6, local copies, waits for them, and re-layouts  13.2 us
    all_to_all x1, starting transfers between devices, per_device(): lax.all_to_all(queries, 'dp', split_axis=2, concat_axis=0, tiled=True)  7.39 us
    all_to_all x1, waiting for transfers between devices, per_device(): lax.all_to_all(queries, 'dp', split_axis=2, concat_axis=0, tiled=True)  5.48 us
    dot_general x1, matrix products, per_device(): jnp.einsum('qlk,lkj->qlj', query_slices, inv_hessian, preferred_element_t...  3.01 us
  transfers between devices with their start and end apart: 1, of which 1 were waited for; matrix products, arithmetic and copies ran while one was open for 0% of the time, Pallas kernels for 0%

commit v1 on v0

v1 whole, which is shorter than its diff:
```python
import functools

import jax
import jax.numpy as jnp
from jax import lax
from jax.experimental import pallas as pl
from jax.experimental.pallas import tpu as pltpu
from jax.sharding import PartitionSpec as P

NT = (((1,), (1,)), ((), ()))


def dot_nt(a, b):
    return lax.dot_general(a, b, NT, preferred_element_type=jnp.float32)


def gather(n, buf, send_sem, recv_sem, me):
    line = n // 4
    z, y, c = me // 4, lax.rem(me // 2, 2), lax.rem(me, 2)

    def index(zz, yy, cc):
        return (zz * 2 + yy) * 2 + cc

    sends = []

    def send(slot, to):
        copy = pltpu.make_async_remote_copy(
            src_ref=buf.at[slot], dst_ref=buf.at[slot],
            send_sem=send_sem.at[len(sends)], recv_sem=recv_sem.at[slot],
            device_id={"dp": to}, device_id_type=pl.DeviceIdType.MESH)
        copy.start()
        sends.append(copy)

    def arrived(slot):
        pltpu.make_async_remote_copy(
            src_ref=buf.at[slot], dst_ref=buf.at[slot],
            send_sem=send_sem.at[0], recv_sem=recv_sem.at[slot],
            device_id={"dp": index(z, y, 1 - c)}, device_id_type=pl.DeviceIdType.MESH).wait_recv()

    zs = [lax.rem(z + d, line) for d in range(line)]
    across, other = index(z, 1 - y, c), index(z, y, 1 - c)
    for d in range(1, line):
        send(me, index(zs[d], y, c))
    send(me, across)
    send(me, other)
    for d in range(1, line):
        slot = index(zs[d], y, c)
        arrived(slot)
        send(slot, across)
        send(slot, other)
    for d in range(line):
        slot = index(zs[d], 1 - y, c)
        arrived(slot)
        send(slot, other)
    yield None
    for d in range(line):
        arrived(index(zs[d], y, 1 - c))
        arrived(index(zs[d], 1 - y, 1 - c))
    yield None
    for copy in sends:
        copy.wait_send()
    yield None


def kernel(n, q_hbm, h_hbm, x_hbm, o_ref, qv, qg, pg, hv, xv, acc, local_sem, qs, qr, ps, pr):
    me = lax.axis_index("dp")
    line = n // 4
    z, y, c = me // 4, lax.rem(me // 2, 2), lax.rem(me, 2)
    nq_local, layers, feats = qv.shape
    nq = nq_local * n
    rows = hv.shape[1]
    width = qg.shape[2]
    parts = feats // width

    load_q = pltpu.make_async_copy(q_hbm, qv, local_sem.at[0])
    load_h = pltpu.make_async_copy(h_hbm, hv, local_sem.at[1])
    load_x = pltpu.make_async_copy(x_hbm.reshape(xv.shape), xv, local_sem.at[2])
    load_q.start()
    load_h.start()
    load_x.start()

    barrier = pltpu.get_barrier_semaphore()
    peers = [(lax.rem(z + d, line) * 2 + y) * 2 + c for d in range(1, line)]
    peers += [(z * 2 + 1 - y) * 2 + c, (z * 2 + y) * 2 + 1 - c]
    for peer in peers:
        pl.semaphore_signal(barrier, inc=1, device_id={"dp": peer}, device_id_type=pl.DeviceIdType.MESH)

    load_q.wait()
    tiles = []
    for i in range(nq_local):
        v = qv[i].astype(jnp.float32)
        tiles.append(jnp.concatenate([v[:, k * width:(k + 1) * width] for k in range(parts)], axis=0))
    qg[me] = jnp.concatenate(tiles, axis=0).astype(jnp.bfloat16)
    pl.semaphore_wait(barrier, len(peers))

    steps = gather(n, qg, qs, qr, me)
    next(steps)
    total = nq * layers * parts
    ri = lax.broadcasted_iota(jnp.int32, (total, total), 0)
    ci = lax.broadcasted_iota(jnp.int32, (total, total), 1)
    pick = (lax.rem(ri, nq) * (layers * parts) + ri // nq == ci).astype(jnp.float32).astype(jnp.bfloat16)
    next(steps)
    load_h.wait()
    ordered = jnp.dot(pick, qg[...].reshape(total, width), preferred_element_type=jnp.float32).astype(jnp.bfloat16)
    for l in range(layers):
        block = jnp.zeros((nq, rows), jnp.float32)
        for k in range(parts):
            first = (k * layers + l) * nq
            block += dot_nt(ordered[first:first + nq], hv[l, :, k * width:(k + 1) * width])
        pg[me, l * nq:(l + 1) * nq, :] = block.astype(jnp.bfloat16)
    next(steps)

    def score(slot):
        cols = pl.ds(pl.multiple_of(slot * rows, rows), rows)
        acc[...] += dot_nt(xv[:, cols], pg[slot])

    steps = gather(n, pg, ps, pr, me)
    next(steps)
    load_x.wait()
    acc[...] = jnp.zeros_like(acc)

    @pl.loop(0, n // 2)
    def _(i):
        score(i * 2 + c)

    next(steps)

    @pl.loop(0, n // 2)
    def _(i):
        score(i * 2 + 1 - c)

    next(steps)
    t = o_ref.shape[1]
    result = acc[pl.ds(0, t, layers), :][:, 0:nq]
    for l in range(1, layers):
        result += acc[pl.ds(l, t, layers), :][:, l * nq:(l + 1) * nq]
    o_ref[...] = result.T


def fused(n, queries, inv_hessian, train_grads):
    nq_local, layers, feats = queries.shape
    rows = inv_hessian.shape[1]
    t = train_grads.shape[0]
    nq = nq_local * n
    held = 16
    width = nq_local * layers * feats // held
    return pl.pallas_call(
        functools.partial(kernel, n),
        out_shape=jax.ShapeDtypeStruct((nq, t), jnp.float32),
        in_specs=[pl.BlockSpec(memory_space=pl.ANY)] * 3,
        out_specs=pl.BlockSpec(memory_space=pltpu.VMEM),
        scratch_shapes=[
            pltpu.VMEM((nq_local, layers, feats), jnp.bfloat16),
            pltpu.VMEM((n, held, width), jnp.bfloat16),
            pltpu.VMEM((n, layers * nq, rows), jnp.bfloat16),
            pltpu.VMEM((layers, rows, feats), jnp.bfloat16),
            pltpu.VMEM((t * layers, feats), jnp.bfloat16),
            pltpu.VMEM((t * layers, layers * nq), jnp.float32),
            pltpu.SemaphoreType.DMA((3,)),
            pltpu.SemaphoreType.DMA((n,)),
            pltpu.SemaphoreType.DMA((n,)),
            pltpu.SemaphoreType.DMA((n,)),
            pltpu.SemaphoreType.DMA((n,)),
        ],
        compiler_params=pltpu.CompilerParams(
            collective_id=0, has_side_effects=True, vmem_limit_bytes=48 * 2**20),
        cost_estimate=pl.CostEstimate(
            flops=2 * nq * layers * feats * (rows + t),
            bytes_accessed=2 * layers * feats * (rows + t), transcendentals=0),
    )(queries, inv_hessian, train_grads)


def plain(queries, inv_hessian, train_grads):
    nq_local, layers, feats = queries.shape
    t = train_grads.shape[0]
    whole = lax.all_gather(queries, "dp", axis=0, tiled=True)
    piece = jnp.einsum("qlj,lrj->qlr", whole, inv_hessian, preferred_element_type=jnp.float32).astype(jnp.bfloat16)
    precond = lax.all_gather(piece, "dp", axis=2, tiled=True)
    return jnp.dot(precond.reshape(-1, layers * feats), train_grads.reshape(t, layers * feats).T,
                   preferred_element_type=jnp.float32)


def solution(mesh):
    n = mesh.shape["dp"]

    def per_device(queries, inv_hessian, train_grads):
        nq_local, layers, feats = queries.shape
        if n == 16 and nq_local == 2 and layers == 2 and feats == 16 * inv_hessian.shape[1]:
            return fused(n, queries, inv_hessian, train_grads)
        return plain(queries, inv_hessian, train_grads)

    return jax.shard_map(
        per_device,
        mesh=mesh,
        in_specs=(P("dp", None, None), P(None, "dp", None), P(("groups", "dp"), None, None)),
        out_specs=P(None, ("groups", "dp")),
        check_vma=False,
    )
```

time: 133 us -> 31.4 us (0.24)
  blocking collectives: 88.2 us -> 0 us
  Pallas kernels: 0 us -> 27.6 us
  matrix products: 16.3 us -> 0 us
  local copies, waits for them, and re-layouts: 14.7 us -> 3.58 us
  starting transfers between devices: 7.39 us -> 0 us
  waiting for transfers between devices: 5.48 us -> 0 us
    unnamed x1 -> x0, blocking collectives: 69.3 us -> none
    pallas_call x0 -> x1, Pallas kernels: none -> 27.6 us  [fused(): pl.pallas_call(functools.partial(kernel, n), out_shape=jax.ShapeDtypeStru...]
    all_gather x1 -> x0, blocking collectives: 18.9 us -> none  [per_device(): gathered_piece = lax.all_gather(precond, 'dp', axis=0, tiled=True)]
    dot_general x2 -> x0, matrix products: 16.3 us -> none  [the longest x1 13.3 us: per_device(): return jnp.dot(flat_piece, train_flat.T, preferred_element_type=jnp.float32)]
    unnamed x6 -> x5, local copies, waits for them, and re-layouts: 13.2 us -> 3.58 us
    all_to_all x1 -> x0, starting transfers between devices: 7.39 us -> none  [per_device(): lax.all_to_all(queries, 'dp', split_axis=2, concat_axis=0, tiled=True)]
    all_to_all x1 -> x0, waiting for transfers between devices: 5.48 us -> none  [per_device(): lax.all_to_all(queries, 'dp', split_axis=2, concat_axis=0, tiled=True)]
    all_to_all x1 -> x0, local copies, waits for them, and re-layouts: 1.34 us -> none  [per_device(): lax.all_to_all(queries, 'dp', split_axis=2, concat_axis=0, tiled=True)]
  transfers between devices with their start and end apart: 1 -> 0, of which waited for: 1 -> 0; matrix products, arithmetic and copies ran while one was open for 0% -> 0% of each run, Pallas kernels for 0% -> 0%
where the time goes in v1:
time: 31.4 us; the launch traced here: 31.1 us
  Pallas kernels  27.6 us (88%)
  local copies, waits for them, and re-layouts  3.58 us (11%)
    pallas_call x1, Pallas kernels, fused(): pl.pallas_call(functools.partial(kernel, n), out_shape=jax.ShapeDtypeStru...  27.6 us
    unnamed x5, local copies, waits for them, and re-layouts  3.58 us

profile of v1, /device:TPU:0, one launch (start us, length us, event | category | flops | bytes accessed | tf_op | source)
XLA Modules:
  0.0 31.1 jit_solution(4520890325490777639)
XLA Ops:
  0.0 0.0 copy-start
  0.0 2.2 %copy-done = bf16[2,256,4096]{2,1,0:T(8,128)(2,1)S(1)} copy-done((bf16[2,256,4096]{2,1,0:T(8,128)(2,1)S(1)}, bf16[2,256,4096]{2,1,0:T(8,128)(2,1)}, u32[]{:S(2)}) %copy-start) | copy-done | bytes 4194328
  2.2 0.0 copy-start.1
  2.2 0.8 %copy-done.1 = bf16[2,2,4096]{2,1,0:T(2,128)(2,1)S(1)} copy-done((bf16[2,2,4096]{2,1,0:T(2,128)(2,1)S(1)}, bf16[2,2,4096]{2,1,0:T(2,128)(2,1)}, u32[]{:S(2)}) %copy-start.1) | copy-done | bytes 32792
  2.9 27.6 %shard_map.37 = f32[32,512]{1,0:T(8,128)S(1)} custom-call(bf16[2,2,4096]{2,1,0:T(2,128)(2,1)S(1)} %copy-done.1, bf16[2,256,4096]{2,1,0:T(8,128)(2,1)S(1)} %copy-done, bf16[512,2,4096]{2,1,0:T(2,128)(2,1)} %x_hbm.1), custom_call_target="tpu_custom_call" | custom-call | flops 402653184 | bytes 12582912 | tf_op jit(solution)/shard_map/pallas_call | solution.py:147
  30.5 0.6 %copy.5 = f32[32,512]{1,0:T(8,128)} copy(f32[32,512]{1,0:T(8,128)S(1)} %shard_map.37) | data formatting | bytes 131072
Async XLA Ops:
  0.0 2.2 %copy-start = (bf16[2,256,4096]{2,1,0:T(8,128)(2,1)S(1)}, bf16[2,256,4096]{2,1,0:T(8,128)(2,1)}, u32[]{:S(2)}) copy-start(bf16[2,256,4096]{2,1,0:T(8,128)(2,1)} %h_hbm.1) | copy-start | bytes 12582916
  2.2 0.8 %copy-start.1 = (bf16[2,2,4096]{2,1,0:T(2,128)(2,1)S(1)}, bf16[2,2,4096]{2,1,0:T(2,128)(2,1)}, u32[]{:S(2)}) copy-start(bf16[2,2,4096]{2,1,0:T(2,128)(2,1)} %q_hbm.1) | copy-start | bytes 98308

commit v2 on v0

v2 whole, which is shorter than its diff:
```python
import functools

import jax
import jax.numpy as jnp
from jax import lax
from jax.experimental import pallas as pl
from jax.experimental.pallas import tpu as pltpu
from jax.sharding import PartitionSpec as P

NT = (((1,), (1,)), ((), ()))


def dot_nt(a, b):
    return lax.dot_general(a, b, NT, preferred_element_type=jnp.float32)


def index(z, y, c):
    return (z * 2 + y) * 2 + c


def place(me):
    z, y, c = me // 4, lax.rem(me // 2, 2), lax.rem(me, 2)
    return [z, z + 1 - 2 * lax.rem(z, 2), lax.rem(z + 2, 4), 3 - z], y, c


class Copies:
    def __init__(self, send_sem, recv_sem):
        self.send_sem, self.recv_sem, self.started = send_sem, recv_sem, []

    def copy(self, ref, arrival, to, k):
        return pltpu.make_async_remote_copy(
            src_ref=ref, dst_ref=ref, send_sem=self.send_sem.at[k], recv_sem=self.recv_sem.at[arrival],
            device_id=to, device_id_type=pl.DeviceIdType.MESH)

    def send(self, ref, arrival, to):
        copy = self.copy(ref, arrival, to, len(self.started))
        copy.start()
        self.started.append(copy)

    def arrived(self, ref, arrival, to):
        self.copy(ref, arrival, to, 0).wait_recv()

    def finish(self):
        for copy in self.started:
            copy.wait_send()


def gather_queries(buf, send_sem, recv_sem, group, me):
    zs, y, c = place(me)
    copies = Copies(send_sem, recv_sem)
    other = {"groups": group, "dp": index(zs[0], y, 1 - c)}
    chips = [(zs[0], 1 - y), (zs[1], y), (zs[1], 1 - y), (zs[2], y), (zs[3], y), (zs[2], 1 - y), (zs[3], 1 - y)]
    for z, yy in reversed(chips):
        copies.send(buf.at[me], me, {"groups": group, "dp": index(z, yy, c)})
    copies.send(buf.at[me], me, other)
    for z, yy in chips:
        slot = index(z, yy, c)
        copies.arrived(buf.at[slot], slot, other)
        copies.send(buf.at[slot], slot, other)
    for z, yy in [(zs[0], y)] + chips:
        slot = index(z, yy, 1 - c)
        copies.arrived(buf.at[slot], slot, other)
    return copies


def gather_precond(n, nq, buf, send_sem, recv_sem, group, me, use):
    zs, y, c = place(me)
    copies = Copies(send_sem, recv_sem)
    other = {"groups": group, "dp": index(zs[0], y, 1 - c)}
    across = {"groups": group, "dp": index(zs[0], 1 - y, c)}

    def half(slot, layer):
        return buf.at[slot, pl.ds(pl.multiple_of(layer * nq, nq), nq)]

    for z in reversed(zs):
        copies.send(half(me, group), group * n + me, {"groups": 1 - group, "dp": index(z, y, c)})
        if z is not zs[0]:
            copies.send(half(me, group), group * n + me, {"groups": group, "dp": index(z, y, c)})

    own = [index(z, y, c) for z in zs]
    far = [index(z, 1 - y, c) for z in zs]
    own_x = [index(z, y, 1 - c) for z in zs]
    far_x = [index(z, 1 - y, 1 - c) for z in zs]

    def take(slot):
        copies.arrived(buf.at[slot], slot, other)

    for j, slot in enumerate(own):
        copies.arrived(half(slot, 1 - group), (1 - group) * n + slot, other)
        if j:
            copies.arrived(half(slot, group), group * n + slot, other)
        copies.send(buf.at[slot], slot, across)
        copies.send(buf.at[slot], slot, other)
        if j:
            use(own[j - 1])
    take(own_x[0])
    use(own[3], own_x[0])
    take(far[0])
    copies.send(buf.at[far[0]], far[0], other)
    take(own_x[1])
    take(own_x[2])
    use(own_x[1], own_x[2])
    take(far[1])
    copies.send(buf.at[far[1]], far[1], other)
    take(own_x[3])
    use(own_x[3], far[0])
    take(far[2])
    copies.send(buf.at[far[2]], far[2], other)
    take(far_x[0])
    use(far[1], far_x[0])
    take(far[3])
    copies.send(buf.at[far[3]], far[3], other)
    take(far_x[1])
    use(far[2], far_x[1])
    take(far_x[2])
    use(far[3], far_x[2])
    take(far_x[3])
    use(far_x[3])
    return copies


def kernel(n, q_hbm, h_hbm, x_hbm, o_ref, qv, qg, pg, hv, xv, acc, local_sem, qs, qr, ps, pr):
    group, me = lax.axis_index("groups"), lax.axis_index("dp")
    nq_local, layers, feats = qv.shape
    nq = nq_local * n
    rows = hv.shape[0]
    width = qg.shape[2]
    parts = feats // width

    load_q = pltpu.make_async_copy(q_hbm, qv, local_sem.at[0])
    load_h = pltpu.make_async_copy(h_hbm.at[group], hv, local_sem.at[1])
    load_x = pltpu.make_async_copy(x_hbm.reshape(xv.shape), xv, local_sem.at[2])
    load_q.start()
    load_h.start()
    load_x.start()

    barrier = pltpu.get_barrier_semaphore()
    zs, y, c = place(me)
    peers = [(group, index(z, yy, c)) for z in zs for yy in (y, 1 - y)][1:]
    peers += [(1 - group, index(z, y, c)) for z in zs] + [(group, index(zs[0], y, 1 - c))]
    for peer in reversed(peers):
        pl.semaphore_signal(barrier, inc=1, device_id={"groups": peer[0], "dp": peer[1]},
                            device_id_type=pl.DeviceIdType.MESH)

    load_q.wait()
    tiles = []
    for i in range(nq_local):
        v = qv[i].astype(jnp.float32)
        v = jnp.where(group == 0, v[0:1], v[1:2])
        tiles += [v[:, k * width:(k + 1) * width] for k in range(parts)]
    qg[me] = jnp.concatenate(tiles, axis=0).astype(jnp.bfloat16)

    total = nq * parts
    ri = lax.broadcasted_iota(jnp.int32, (total, total), 0)
    ci = lax.broadcasted_iota(jnp.int32, (total, total), 1)
    pick = (lax.rem(ri, nq) * parts + ri // nq == ci).astype(jnp.float32).astype(jnp.bfloat16)
    acc[...] = jnp.zeros_like(acc)
    pl.semaphore_wait(barrier, len(peers))

    queries = gather_queries(qg, qs, qr, group, me)
    load_h.wait()
    ordered = jnp.dot(pick, qg[...].reshape(total, width), preferred_element_type=jnp.float32).astype(jnp.bfloat16)
    block = jnp.zeros((nq, rows), jnp.float32)
    for k in range(parts):
        block += dot_nt(ordered[k * nq:(k + 1) * nq], hv[:, k * width:(k + 1) * width])
    pg[me, pl.ds(pl.multiple_of(group * nq, nq), nq), :] = block.astype(jnp.bfloat16)
    load_x.wait()

    def score(*slots):
        acc[...] += sum(dot_nt(xv[:, pl.ds(pl.multiple_of(s * rows, rows), rows)], pg[s]) for s in slots)

    precond = gather_precond(n, nq, pg, ps, pr, group, me, score)
    t = o_ref.shape[1]
    result = acc[pl.ds(0, t, layers), :][:, 0:nq]
    for l in range(1, layers):
        result += acc[pl.ds(l, t, layers), :][:, l * nq:(l + 1) * nq]
    o_ref[...] = result.T
    queries.finish()
    precond.finish()


def fused(n, queries, inv_hessian, train_grads):
    nq_local, layers, feats = queries.shape
    rows = inv_hessian.shape[1]
    t = train_grads.shape[0]
    nq = nq_local * n
    held = 16
    width = nq_local * feats // held
    return pl.pallas_call(
        functools.partial(kernel, n),
        out_shape=jax.ShapeDtypeStruct((nq, t), jnp.float32),
        in_specs=[pl.BlockSpec(memory_space=pltpu.HBM)] * 3,
        out_specs=pl.BlockSpec(memory_space=pltpu.VMEM),
        scratch_shapes=[
            pltpu.VMEM((nq_local, layers, feats), jnp.bfloat16),
            pltpu.VMEM((n, held, width), jnp.bfloat16),
            pltpu.VMEM((n, layers * nq, rows), jnp.bfloat16),
            pltpu.VMEM((rows, feats), jnp.bfloat16),
            pltpu.VMEM((t * layers, feats), jnp.bfloat16),
            pltpu.VMEM((t * layers, layers * nq), jnp.float32),
            pltpu.SemaphoreType.DMA((3,)),
            pltpu.SemaphoreType.DMA((n,)),
            pltpu.SemaphoreType.DMA((n,)),
            pltpu.SemaphoreType.DMA((2 * n,)),
            pltpu.SemaphoreType.DMA((2 * n,)),
        ],
        compiler_params=pltpu.CompilerParams(
            collective_id=0, has_side_effects=True, vmem_limit_bytes=60 * 2**20),
        cost_estimate=pl.CostEstimate(
            flops=2 * nq * feats * (rows + layers * t),
            bytes_accessed=2 * feats * (rows + layers * t), transcendentals=0),
    )(queries, inv_hessian, train_grads)


def plain(queries, inv_hessian, train_grads):
    nq_local, layers, feats = queries.shape
    t = train_grads.shape[0]
    whole = lax.all_gather(queries, "dp", axis=0, tiled=True)
    piece = jnp.einsum("qlj,lrj->qlr", whole, inv_hessian, preferred_element_type=jnp.float32).astype(jnp.bfloat16)
    precond = lax.all_gather(piece, "dp", axis=2, tiled=True)
    return jnp.dot(precond.reshape(-1, layers * feats), train_grads.reshape(t, layers * feats).T,
                   preferred_element_type=jnp.float32)


def solution(mesh):
    n = mesh.shape["dp"]

    def per_device(queries, inv_hessian, train_grads):
        nq_local, layers, feats = queries.shape
        if n == 16 and mesh.shape["groups"] == 2 and nq_local == 2 and layers == 2 and feats == 16 * inv_hessian.shape[1]:
            return fused(n, queries, inv_hessian, train_grads)
        return plain(queries, inv_hessian, train_grads)

    return jax.shard_map(
        per_device,
        mesh=mesh,
        in_specs=(P("dp", None, None), P(None, "dp", None), P(("groups", "dp"), None, None)),
        out_specs=P(None, ("groups", "dp")),
        check_vma=False,
    )
```

time: 133 us -> 24.6 us (0.18)
  blocking collectives: 88.2 us -> 0 us
  Pallas kernels: 0 us -> 22.9 us
  matrix products: 16.3 us -> 0 us
  local copies, waits for them, and re-layouts: 14.7 us -> 1.47 us
  starting transfers between devices: 7.39 us -> 0 us
  waiting for transfers between devices: 5.48 us -> 0 us
    unnamed x1 -> x0, blocking collectives: 69.3 us -> none
    pallas_call x0 -> x1, Pallas kernels: none -> 22.9 us  [fused(): pl.pallas_call(functools.partial(kernel, n), out_shape=jax.ShapeDtypeStru...]
    all_gather x1 -> x0, blocking collectives: 18.9 us -> none  [per_device(): gathered_piece = lax.all_gather(precond, 'dp', axis=0, tiled=True)]
    dot_general x2 -> x0, matrix products: 16.3 us -> none  [the longest x1 13.3 us: per_device(): return jnp.dot(flat_piece, train_flat.T, preferred_element_type=jnp.float32)]
    unnamed x6 -> x1, local copies, waits for them, and re-layouts: 13.2 us -> 1.47 us
    all_to_all x1 -> x0, starting transfers between devices: 7.39 us -> none  [per_device(): lax.all_to_all(queries, 'dp', split_axis=2, concat_axis=0, tiled=True)]
    all_to_all x1 -> x0, waiting for transfers between devices: 5.48 us -> none  [per_device(): lax.all_to_all(queries, 'dp', split_axis=2, concat_axis=0, tiled=True)]
    all_to_all x1 -> x0, local copies, waits for them, and re-layouts: 1.34 us -> none  [per_device(): lax.all_to_all(queries, 'dp', split_axis=2, concat_axis=0, tiled=True)]
  transfers between devices with their start and end apart: 1 -> 0, of which waited for: 1 -> 0; matrix products, arithmetic and copies ran while one was open for 0% -> 0% of each run, Pallas kernels for 0% -> 0%
where the time goes in v2:
time: 24.6 us; the launch traced here: 24.4 us
  Pallas kernels  22.9 us (93%)
  local copies, waits for them, and re-layouts  1.47 us (6%)
    pallas_call x1, Pallas kernels, fused(): pl.pallas_call(functools.partial(kernel, n), out_shape=jax.ShapeDtypeStru...  22.9 us
    unnamed x1, local copies, waits for them, and re-layouts  1.47 us

profile of v2, /device:TPU:0, one launch (start us, length us, event | category | flops | bytes accessed | tf_op | source)
XLA Modules:
  0.0 24.4 jit_solution(9160090837139027130)
XLA Ops:
  0.0 22.9 %shard_map.37 = f32[32,512]{1,0:T(8,128)} custom-call(bf16[2,2,4096]{2,1,0:T(2,128)(2,1)} %q_hbm.1, bf16[2,256,4096]{2,1,0:T(8,128)(2,1)} %h_hbm.1, bf16[512,2,4096]{2,1,0:T(2,128)(2,1)} %x_hbm.1), custom_call_target="tpu_custom_call" | custom-call | flops 335544320 | bytes 10485760 | tf_op jit(solution)/shard_map/pallas_call | solution.py:189
  22.9 1.5 %copy.5 = f32[32,512]{1,0:T(8,128)} copy(f32[32,512]{1,0:T(8,128)} %shard_map.37) | data formatting | bytes 131072

commit v3 on v2

--- a/solution.py
+++ b/solution.py
@@ -72,10 +72,10 @@
     def half(slot, layer):
         return buf.at[slot, pl.ds(pl.multiple_of(layer * nq, nq), nq)]
 
-    for z in reversed(zs):
+    for z in zs:
         copies.send(half(me, group), group * n + me, {"groups": 1 - group, "dp": index(z, y, c)})
-        if z is not zs[0]:
-            copies.send(half(me, group), group * n + me, {"groups": group, "dp": index(z, y, c)})
+    for z in reversed(zs[1:]):
+        copies.send(half(me, group), group * n + me, {"groups": group, "dp": index(z, y, c)})
 
     own = [index(z, y, c) for z in zs]
     far = [index(z, 1 - y, c) for z in zs]
@@ -119,7 +119,7 @@
     return copies
 
 
-def kernel(n, q_hbm, h_hbm, x_hbm, o_ref, qv, qg, pg, hv, xv, acc, local_sem, qs, qr, ps, pr):
+def kernel(n, qv, h_hbm, x_hbm, o_ref, qg, pg, hv, xv, acc, local_sem, qs, qr, ps, pr):
     group, me = lax.axis_index("groups"), lax.axis_index("dp")
     nq_local, layers, feats = qv.shape
     nq = nq_local * n
@@ -127,10 +127,8 @@
     width = qg.shape[2]
     parts = feats // width
 
-    load_q = pltpu.make_async_copy(q_hbm, qv, local_sem.at[0])
-    load_h = pltpu.make_async_copy(h_hbm.at[group], hv, local_sem.at[1])
-    load_x = pltpu.make_async_copy(x_hbm.reshape(xv.shape), xv, local_sem.at[2])
-    load_q.start()
+    load_h = pltpu.make_async_copy(h_hbm.at[group], hv, local_sem.at[0])
+    load_x = pltpu.make_async_copy(x_hbm.reshape(xv.shape), xv, local_sem.at[1])
     load_h.start()
     load_x.start()
 
@@ -142,7 +140,6 @@
         pl.semaphore_signal(barrier, inc=1, device_id={"groups": peer[0], "dp": peer[1]},
                             device_id_type=pl.DeviceIdType.MESH)
 
-    load_q.wait()
     tiles = []
     for i in range(nq_local):
         v = qv[i].astype(jnp.float32)
@@ -189,23 +186,22 @@
     return pl.pallas_call(
         functools.partial(kernel, n),
         out_shape=jax.ShapeDtypeStruct((nq, t), jnp.float32),
-        in_specs=[pl.BlockSpec(memory_space=pltpu.HBM)] * 3,
+        in_specs=[pl.BlockSpec(memory_space=pltpu.VMEM)] + [pl.BlockSpec(memory_space=pltpu.HBM)] * 2,
         out_specs=pl.BlockSpec(memory_space=pltpu.VMEM),
         scratch_shapes=[
-            pltpu.VMEM((nq_local, layers, feats), jnp.bfloat16),
             pltpu.VMEM((n, held, width), jnp.bfloat16),
             pltpu.VMEM((n, layers * nq, rows), jnp.bfloat16),
             pltpu.VMEM((rows, feats), jnp.bfloat16),
             pltpu.VMEM((t * layers, feats), jnp.bfloat16),
             pltpu.VMEM((t * layers, layers * nq), jnp.float32),
-            pltpu.SemaphoreType.DMA((3,)),
+            pltpu.SemaphoreType.DMA((2,)),
             pltpu.SemaphoreType.DMA((n,)),
             pltpu.SemaphoreType.DMA((n,)),
             pltpu.SemaphoreType.DMA((2 * n,)),
             pltpu.SemaphoreType.DMA((2 * n,)),
         ],
         compiler_params=pltpu.CompilerParams(
-            collective_id=0, has_side_effects=True, vmem_limit_bytes=60 * 2**20),
+            collective_id=0, has_side_effects=True, vmem_limit_bytes=53 * 2**20),
         cost_estimate=pl.CostEstimate(
             flops=2 * nq * feats * (rows + layers * t),
             bytes_accessed=2 * feats * (rows + layers * t), transcendentals=0),

time: 24.6 us -> 23.9 us (0.972)
  Pallas kernels: 22.9 us -> 22.3 us
    pallas_call x1, Pallas kernels: 22.9 us -> 22.3 us  [fused(): pl.pallas_call(functools.partial(kernel, n), out_shape=jax.ShapeDtypeStru...]
    unnamed x1 -> x3, local copies, waits for them, and re-layouts: 1.47 us -> 1.39 us
where the time goes in v3:
time: 23.9 us; the launch traced here: 23.7 us
  Pallas kernels  22.3 us (93%)
  local copies, waits for them, and re-layouts  1.39 us (6%)
    pallas_call x1, Pallas kernels, fused(): pl.pallas_call(functools.partial(kernel, n), out_shape=jax.ShapeDtypeStru...  22.3 us
    unnamed x3, local copies, waits for them, and re-layouts  1.39 us

profile of v3, /device:TPU:0, one launch (start us, length us, event | category | flops | bytes accessed | tf_op | source)
XLA Modules:
  0.0 23.7 jit_solution(6951242750940483365)
XLA Ops:
  0.0 0.0 copy-start
  0.0 0.8 %copy-done = bf16[2,2,4096]{2,1,0:T(2,128)(2,1)S(1)} copy-done((bf16[2,2,4096]{2,1,0:T(2,128)(2,1)S(1)}, bf16[2,2,4096]{2,1,0:T(2,128)(2,1)}, u32[]{:S(2)}) %copy-start) | copy-done | bytes 32792
  0.8 22.3 %shard_map.37 = f32[32,512]{1,0:T(8,128)S(1)} custom-call(bf16[2,2,4096]{2,1,0:T(2,128)(2,1)S(1)} %copy-done, bf16[2,256,4096]{2,1,0:T(8,128)(2,1)} %h_hbm.1, bf16[512,2,4096]{2,1,0:T(2,128)(2,1)} %x_hbm.1), custom_call_target="tpu_custom_call" | custom-call | flops 335544320 | bytes 10485760 | tf_op jit(solution)/shard_map/pallas_call | solution.py:186
  23.1 0.6 %copy.5 = f32[32,512]{1,0:T(8,128)} copy(f32[32,512]{1,0:T(8,128)S(1)} %shard_map.37) | data formatting | bytes 131072
Async XLA Ops:
  0.0 0.8 %copy-start = (bf16[2,2,4096]{2,1,0:T(2,128)(2,1)S(1)}, bf16[2,2,4096]{2,1,0:T(2,128)(2,1)}, u32[]{:S(2)}) copy-start(bf16[2,2,4096]{2,1,0:T(2,128)(2,1)} %qv.1) | copy-start | bytes 98308
